TPU v7x, 32 devices: a whole 2x2x4 slice. The times are simulated.
32 devices in a mesh: groups: 2 (over x), chan: 16 (over z, y, core).
Axes of the slice: x: 2, y: 2, z: 4, core: 2. Of those that a mesh axis runs over, the one named last changes fastest.
Arguments:
- samples: bfloat16 [2048, 638], P(('groups', 'chan')), parts along dimension 0, may hold values from -6 to 6
- templates: bfloat16 [16, 64, 256], P('chan'), may hold values from -0.046875 to 0.046875
- moveouts: int32 [16, 64], P('chan'), may hold values from 0 to 255
- offsets: int32 [16], P('chan'), may hold values from 0 to 63, as said below
Outputs:
- stacks: float32 [32, 16, 128], P(('groups', 'chan')), parts along dimension 0
There are 2 independent parts, one for each index of `groups`. A program takes and returns all parts, laid end to end along the dimension named above; an argument that names none is the same for every part. Nothing has to cross between parts.
Inputs may be any that keep to these rules, and one draw needn't show every extreme that they name: `offsets`: offset of a template's first channel from the start of a block of 64 channels; both 0 and 63 occur.
All inputs are finite; a program needn't handle non-finite values.
Results may differ from a plain program's by a relative error of at most 0.0003.
Values may be sent and summed in bfloat16 or wider, within the bound.
A program may use at most 64 MiB of HBM per device.

v0:
```python
import jax
import jax.numpy as jnp
from jax import lax
from jax.sharding import PartitionSpec as P

MOVE = 256


def from_behind(value, axis, steps):
    count = lax.axis_size(axis)
    initial, last = (max(0, -steps), min(count, count - steps))
    return lax.ppermute(value, axis, [(source, source + steps) for source in range(initial, last)])


def correlate(signal, kernel):
    result = lax.conv_general_dilated(
        signal,
        kernel[None],
        (1,),
        "VALID",
        dimension_numbers=("NCH", "OIH", "NCH"),
        preferred_element_type=jnp.float32,
    )
    return result[:, 0]


def per_device(samples, templates, moveouts, offsets):
    block_rows = samples.shape[0]
    slab_length = samples.shape[1]
    tap_count = templates.shape[2]
    lag_count = slab_length - tap_count - MOVE + 2
    template_total = templates.shape[0] * lax.axis_size("chan")
    spare = jnp.zeros((block_rows - 1, slab_length), samples.dtype)
    leading = jnp.zeros((block_rows, slab_length), samples.dtype)
    blocks = jnp.stack(
        [
            jnp.concatenate([samples, spare], 0),
            jnp.concatenate([leading, samples[: block_rows - 1]], 0),
        ]
    )

    def shift_signal(signal, amount):
        return lax.dynamic_slice_in_dim(signal, amount, lag_count + tap_count - 1, 0)

    def single_template(entry):
        pattern, delays, offset = entry
        windows = lax.dynamic_slice_in_dim(blocks, offset, block_rows, 1)
        shifted = jax.vmap(lambda window: jax.vmap(shift_signal)(window, delays))(windows)
        return correlate(shifted, pattern)

    initial = jnp.zeros((template_total, blocks.shape[0], lag_count), jnp.float32)
    found = lax.map(
        single_template,
        (
            lax.all_gather(templates, "chan", axis=0, tiled=True),
            lax.all_gather(moveouts, "chan", axis=0, tiled=True),
            lax.all_gather(offsets, "chan", axis=0, tiled=True),
        ),
    )
    total = lax.dynamic_update_slice_in_dim(initial, found, jnp.int32(0), 0)
    nearby = total[:, 0]
    remote = from_behind(total[:, 1], "chan", -1)
    result = nearby + remote
    return result[None]


def solution(mesh):
    in_specs = (P(("groups", "chan"), None), P("chan", None, None), P("chan", None), P("chan"))
    out_specs = P(("groups", "chan"), None, None)
    return jax.shard_map(
        per_device, mesh=mesh, in_specs=in_specs, out_specs=out_specs, check_vma=False
    )
```

profile of v0, /device:TPU:1, one launch (start us, length us, event | category | flops | bytes accessed | tf_op | source)
XLA Modules:
  0.0 1780.6 jit_solution(211351449311182367)
XLA Ops:
  1.0 24.7 %all_gather.11 = bf16[16,64,256]{2,1,0:T(8,128)(2,1)S(1)} all-gather(bf16[1,64,256]{2,1,0:T(8,128)(2,1)} %param.7), channel_id=1, replica_groups=mesh['groups'=2,'chan'=16] {'chan'}, dimensions={0}, use_global_device_ids=true | all-gather | bytes 557056 | tf_op jit(solution)/shard_map/all_gather | solution.py:55
  52.6 1720.8 %while.10 = (s32[]{:T(128)}, f32[16,2,128]{2,0,1:T(8,128)S(1)}, s32[16]{0:T(128)S(1)}, bf16[2,127,638]{2,1,0:T(8,128)(2,1)S(1)}, s32[16,64]{1,0:T(8,128)S(1)}, /...) while((s32[]{:T(128)}, f32[16,2,128]{2,0,1:T(8,128)S(1)}, s32[16]{0:T(128)S(1)}, ...), condition=%wide.region_1.2_spmd, body=%wide.region_0.1_spmd.sunk | while | flops 8389125 | bytes 1117595 | solution.py:52
  64.1 24.0 %gather_fusion = bf16[64,2,383]{1,0,2:T(8,128)(2,1)} fusion(bf16[2,64,638]{0,1,2:T(8,128)(2,1)} %copy.25, s32[64]{0:T(128)S(1)} %or_bitcast_fusion.2), kind=kCustom, calls=%fused_computation.clone.1 | custom fusion | bytes 196608 | tf_op jit(solution)/shard_map/while/body/eval_jaxpr/vmap(vmap())/gather | solution.py:43
  88.2 71.9 %fusion.10 = f32[2,1,128]{0,1,2:T(1,128)S(1)} fusion(bf16[64,2,383]{1,0,2:T(8,128)(2,1)} %gather_fusion, bf16[1,64,256]{1,0,2:T(2,128)(2,1)S(1)} %copy.26), kind=kOutput, calls=%fused_computation.13.clone.1 | convolution fusion | flops 8388608 | bytes 131840 | tf_op jit(solution)/shard_map/while/body/eval_jaxpr/conv_general_dilated | solution.py:16
  171.6 24.0 %gather_fusion = bf16[64,2,383]{1,0,2:T(8,128)(2,1)} fusion(bf16[2,64,638]{0,1,2:T(8,128)(2,1)} %copy.25, s32[64]{0:T(128)S(1)} %or_bitcast_fusion.2), kind=kCustom, calls=%fused_computation.clone.1 | custom fusion | bytes 196608 | tf_op jit(solution)/shard_map/while/body/eval_jaxpr/vmap(vmap())/gather | solution.py:43
  195.7 71.9 %fusion.10 = f32[2,1,128]{0,1,2:T(1,128)S(1)} fusion(bf16[64,2,383]{1,0,2:T(8,128)(2,1)} %gather_fusion, bf16[1,64,256]{1,0,2:T(2,128)(2,1)S(1)} %copy.26), kind=kOutput, calls=%fused_computation.13.clone.1 | convolution fusion | flops 8388608 | bytes 131840 | tf_op jit(solution)/shard_map/while/body/eval_jaxpr/conv_general_dilated | solution.py:16
  303.3 71.9 %fusion.10 = f32[2,1,128]{0,1,2:T(1,128)S(1)} fusion(bf16[64,2,383]{1,0,2:T(8,128)(2,1)} %gather_fusion, bf16[1,64,256]{1,0,2:T(2,128)(2,1)S(1)} %copy.26), kind=kOutput, calls=%fused_computation.13.clone.1 | convolution fusion | flops 8388608 | bytes 131840 | tf_op jit(solution)/shard_map/while/body/eval_jaxpr/conv_general_dilated | solution.py:16
  386.7 24.0 %gather_fusion = bf16[64,2,383]{1,0,2:T(8,128)(2,1)} fusion(bf16[2,64,638]{0,1,2:T(8,128)(2,1)} %copy.25, s32[64]{0:T(128)S(1)} %or_bitcast_fusion.2), kind=kCustom, calls=%fused_computation.clone.1 | custom fusion | bytes 196608 | tf_op jit(solution)/shard_map/while/body/eval_jaxpr/vmap(vmap())/gather | solution.py:43
  410.9 71.9 %fusion.10 = f32[2,1,128]{0,1,2:T(1,128)S(1)} fusion(bf16[64,2,383]{1,0,2:T(8,128)(2,1)} %gather_fusion, bf16[1,64,256]{1,0,2:T(2,128)(2,1)S(1)} %copy.26), kind=kOutput, calls=%fused_computation.13.clone.1 | convolution fusion | flops 8388608 | bytes 131840 | tf_op jit(solution)/shard_map/while/body/eval_jaxpr/conv_general_dilated | solution.py:16
  494.3 24.0 %gather_fusion = bf16[64,2,383]{1,0,2:T(8,128)(2,1)} fusion(bf16[2,64,638]{0,1,2:T(8,128)(2,1)} %copy.25, s32[64]{0:T(128)S(1)} %or_bitcast_fusion.2), kind=kCustom, calls=%fused_computation.clone.1 | custom fusion | bytes 196608 | tf_op jit(solution)/shard_map/while/body/eval_jaxpr/vmap(vmap())/gather | solution.py:43
  518.4 71.9 %fusion.10 = f32[2,1,128]{0,1,2:T(1,128)S(1)} fusion(bf16[64,2,383]{1,0,2:T(8,128)(2,1)} %gather_fusion, bf16[1,64,256]{1,0,2:T(2,128)(2,1)S(1)} %copy.26), kind=kOutput, calls=%fused_computation.13.clone.1 | convolution fusion | flops 8388608 | bytes 131840 | tf_op jit(solution)/shard_map/while/body/eval_jaxpr/conv_general_dilated | solution.py:16
  601.8 24.0 %gather_fusion = bf16[64,2,383]{1,0,2:T(8,128)(2,1)} fusion(bf16[2,64,638]{0,1,2:T(8,128)(2,1)} %copy.25, s32[64]{0:T(128)S(1)} %or_bitcast_fusion.2), kind=kCustom, calls=%fused_computation.clone.1 | custom fusion | bytes 196608 | tf_op jit(solution)/shard_map/while/body/eval_jaxpr/vmap(vmap())/gather | solution.py:43
  626.0 71.9 %fusion.10 = f32[2,1,128]{0,1,2:T(1,128)S(1)} fusion(bf16[64,2,383]{1,0,2:T(8,128)(2,1)} %gather_fusion, bf16[1,64,256]{1,0,2:T(2,128)(2,1)S(1)} %copy.26), kind=kOutput, calls=%fused_computation.13.clone.1 | convolution fusion | flops 8388608 | bytes 131840 | tf_op jit(solution)/shard_map/while/body/eval_jaxpr/conv_general_dilated | solution.py:16
  709.4 24.0 %gather_fusion = bf16[64,2,383]{1,0,2:T(8,128)(2,1)} fusion(bf16[2,64,638]{0,1,2:T(8,128)(2,1)} %copy.25, s32[64]{0:T(128)S(1)} %or_bitcast_fusion.2), kind=kCustom, calls=%fused_computation.clone.1 | custom fusion | bytes 196608 | tf_op jit(solution)/shard_map/while/body/eval_jaxpr/vmap(vmap())/gather | solution.py:43
  733.5 71.9 %fusion.10 = f32[2,1,128]{0,1,2:T(1,128)S(1)} fusion(bf16[64,2,383]{1,0,2:T(8,128)(2,1)} %gather_fusion, bf16[1,64,256]{1,0,2:T(2,128)(2,1)S(1)} %copy.26), kind=kOutput, calls=%fused_computation.13.clone.1 | convolution fusion | flops 8388608 | bytes 131840 | tf_op jit(solution)/shard_map/while/body/eval_jaxpr/conv_general_dilated | solution.py:16
  841.1 71.9 %fusion.10 = f32[2,1,128]{0,1,2:T(1,128)S(1)} fusion(bf16[64,2,383]{1,0,2:T(8,128)(2,1)} %gather_fusion, bf16[1,64,256]{1,0,2:T(2,128)(2,1)S(1)} %copy.26), kind=kOutput, calls=%fused_computation.13.clone.1 | convolution fusion | flops 8388608 | bytes 131840 | tf_op jit(solution)/shard_map/while/body/eval_jaxpr/conv_general_dilated | solution.py:16
  948.6 71.9 %fusion.10 = f32[2,1,128]{0,1,2:T(1,128)S(1)} fusion(bf16[64,2,383]{1,0,2:T(8,128)(2,1)} %gather_fusion, bf16[1,64,256]{1,0,2:T(2,128)(2,1)S(1)} %copy.26), kind=kOutput, calls=%fused_computation.13.clone.1 | convolution fusion | flops 8388608 | bytes 131840 | tf_op jit(solution)/shard_map/while/body/eval_jaxpr/conv_general_dilated | solution.py:16
  1056.2 71.9 %fusion.10 = f32[2,1,128]{0,1,2:T(1,128)S(1)} fusion(bf16[64,2,383]{1,0,2:T(8,128)(2,1)} %gather_fusion, bf16[1,64,256]{1,0,2:T(2,128)(2,1)S(1)} %copy.26), kind=kOutput, calls=%fused_computation.13.clone.1 | convolution fusion | flops 8388608 | bytes 131840 | tf_op jit(solution)/shard_map/while/body/eval_jaxpr/conv_general_dilated | solution.py:16
  1163.7 71.9 %fusion.10 = f32[2,1,128]{0,1,2:T(1,128)S(1)} fusion(bf16[64,2,383]{1,0,2:T(8,128)(2,1)} %gather_fusion, bf16[1,64,256]{1,0,2:T(2,128)(2,1)S(1)} %copy.26), kind=kOutput, calls=%fused_computation.13.clone.1 | convolution fusion | flops 8388608 | bytes 131840 | tf_op jit(solution)/shard_map/while/body/eval_jaxpr/conv_general_dilated | solution.py:16
  1271.3 71.9 %fusion.10 = f32[2,1,128]{0,1,2:T(1,128)S(1)} fusion(bf16[64,2,383]{1,0,2:T(8,128)(2,1)} %gather_fusion, bf16[1,64,256]{1,0,2:T(2,128)(2,1)S(1)} %copy.26), kind=kOutput, calls=%fused_computation.13.clone.1 | convolution fusion | flops 8388608 | bytes 131840 | tf_op jit(solution)/shard_map/while/body/eval_jaxpr/conv_general_dilated | solution.py:16
  1378.8 71.9 %fusion.10 = f32[2,1,128]{0,1,2:T(1,128)S(1)} fusion(bf16[64,2,383]{1,0,2:T(8,128)(2,1)} %gather_fusion, bf16[1,64,256]{1,0,2:T(2,128)(2,1)S(1)} %copy.26), kind=kOutput, calls=%fused_computation.13.clone.1 | convolution fusion | flops 8388608 | bytes 131840 | tf_op jit(solution)/shard_map/while/body/eval_jaxpr/conv_general_dilated | solution.py:16
  1486.4 71.9 %fusion.10 = f32[2,1,128]{0,1,2:T(1,128)S(1)} fusion(bf16[64,2,383]{1,0,2:T(8,128)(2,1)} %gather_fusion, bf16[1,64,256]{1,0,2:T(2,128)(2,1)S(1)} %copy.26), kind=kOutput, calls=%fused_computation.13.clone.1 | convolution fusion | flops 8388608 | bytes 131840 | tf_op jit(solution)/shard_map/while/body/eval_jaxpr/conv_general_dilated | solution.py:16
  1593.9 71.9 %fusion.10 = f32[2,1,128]{0,1,2:T(1,128)S(1)} fusion(bf16[64,2,383]{1,0,2:T(8,128)(2,1)} %gather_fusion, bf16[1,64,256]{1,0,2:T(2,128)(2,1)S(1)} %copy.26), kind=kOutput, calls=%fused_computation.13.clone.1 | convolution fusion | flops 8388608 | bytes 131840 | tf_op jit(solution)/shard_map/while/body/eval_jaxpr/conv_general_dilated | solution.py:16
  1701.5 71.9 %fusion.10 = f32[2,1,128]{0,1,2:T(1,128)S(1)} fusion(bf16[64,2,383]{1,0,2:T(8,128)(2,1)} %gather_fusion, bf16[1,64,256]{1,0,2:T(2,128)(2,1)S(1)} %copy.26), kind=kOutput, calls=%fused_computation.13.clone.1 | convolution fusion | flops 8388608 | bytes 131840 | tf_op jit(solution)/shard_map/while/body/eval_jaxpr/conv_general_dilated | solution.py:16
  (150 shorter events, 433.8 us)
Async XLA Ops:
  1773.5 6.5 collective-permute-start
where the time goes:
time: 1780 us
  matrix products  1150 us (65%)
  local copies, waits for them, and re-layouts  546 us (31%)
  blocking collectives  48.9 us (3%)
  loops' own time  27.6 us (2%)
    conv_general_dilated x16, matrix products, correlate(): lax.conv_general_dilated(signal, kernel[None], (1,), 'VALID', dimension_n...  1150 us
    gather x16, local copies, waits for them, and re-layouts, shift_signal(): lax.dynamic_slice_in_dim(signal, amount, lag_count + tap_count - 1, 0)  384 us
    dynamic_slice x32, local copies, waits for them, and re-layouts, single_template(): windows = lax.dynamic_slice_in_dim(blocks, offset, block_rows, 1)  146 us
  transfers between devices with their start and end apart: 1, of which 1 were waited for; matrix products, arithmetic and copies ran while one was open for 0% of the time, Pallas kernels for 0%

commit v1 on v0

v1 whole, which is shorter than its diff:
```python
import functools

import jax
import jax.numpy as jnp
from jax import lax
from jax.experimental import pallas as pl
from jax.experimental.pallas import tpu as pltpu
from jax.sharding import PartitionSpec as P

MOVE = 256
LANES = 128
ROWS = 16


def kernel(count, x_ref, h_ref, m_ref, off_ref, o_ref,
           buf, shifted, hankel, wide, r_out, r_in,
           a_send, a_recv, b_send, b_recv, r_send, r_recv):
    win, slab = x_ref.shape
    taps = h_ref.shape[2]
    chips = count // 2
    span = taps + MOVE
    padded = shifted.shape[0] * LANES
    packed_rows = buf.shape[1]
    me = lax.axis_index("chan")
    chip, core = me // 2, lax.rem(me, 2)
    sibling = 2 * chip + 1 - core
    before, after = lax.rem(me + count - 1, count), lax.rem(me + 1, count)
    across = lax.rem(me + 2 * core + count - 1, count)

    def far(step):
        return 2 * lax.rem(chip + step, chips) + core

    def near(step):
        return 2 * lax.rem(chip + chips - step, chips) + core

    barrier = pltpu.get_barrier_semaphore()
    pl.semaphore_signal(barrier, inc=1, device_id={"chan": sibling})
    pl.semaphore_signal(barrier, inc=1, device_id={"chan": across})

    @pl.loop(1, chips)
    def _(step):
        pl.semaphore_signal(barrier, inc=1, device_id={"chan": far(step)})

    offset = off_ref[0]
    row = lax.broadcasted_iota(jnp.int32, (win, win), 0)
    col = lax.broadcasted_iota(jnp.int32, (win, win), 1)
    turn = ((row - offset + win) % win == col).astype(jnp.float32).astype(jnp.bfloat16)
    buf[me, 0:win, :] = jnp.dot(turn, h_ref[0], preferred_element_type=jnp.float32).astype(jnp.bfloat16)
    row = lax.broadcasted_iota(jnp.int32, (win, LANES), 0)
    col = lax.broadcasted_iota(jnp.int32, (win, LANES), 1)
    turn = ((row == (col - offset + win) % win) & (col < win)).astype(jnp.float32).astype(jnp.bfloat16)
    moves = jnp.broadcast_to(m_ref[...].astype(jnp.float32), (ROWS, win)).astype(jnp.bfloat16)
    moves = jnp.dot(moves, turn, preferred_element_type=jnp.float32)
    lane = lax.broadcasted_iota(jnp.int32, (ROWS, LANES), 1)
    moves = jnp.where(lane == win, offset.astype(jnp.float32), moves)
    buf[me, win:packed_rows, 0:LANES] = moves.astype(jnp.bfloat16)
    buf[me, win:packed_rows, LANES:taps] = jnp.zeros((ROWS, taps - LANES), jnp.bfloat16)

    pl.semaphore_wait(barrier, chips + 1)

    def to_chip(step):
        return pltpu.make_async_remote_copy(
            src_ref=buf.at[me], dst_ref=buf.at[me], send_sem=a_send.at[step], recv_sem=a_recv.at[step],
            device_id={"chan": far(step)})

    def from_chip(step):
        return pltpu.make_async_remote_copy(
            src_ref=buf.at[near(step)], dst_ref=buf.at[near(step)], send_sem=a_send.at[step],
            recv_sem=a_recv.at[step], device_id={"chan": far(step)})

    def to_sibling(step):
        return pltpu.make_async_remote_copy(
            src_ref=buf.at[near(step)], dst_ref=buf.at[near(step)], send_sem=b_send.at[step],
            recv_sem=b_recv.at[step], device_id={"chan": sibling})

    def from_sibling(step):
        slot = near(step) + 1 - 2 * core
        return pltpu.make_async_remote_copy(
            src_ref=buf.at[slot], dst_ref=buf.at[slot], send_sem=b_send.at[step],
            recv_sem=b_recv.at[step], device_id={"chan": sibling})

    @pl.loop(1, chips)
    def _(step):
        to_chip(step).start()

    to_sibling(0).start()

    samples = jnp.concatenate(
        [x_ref[...].astype(jnp.float32), jnp.zeros((win, padded - slab), jnp.float32)], 1)
    for r in range(ROWS):
        moved = samples if r == 0 else pltpu.roll(samples, padded - r, 1)
        for a in range(padded // LANES):
            shifted[a, r * win:(r + 1) * win, :] = moved[:, a * LANES:(a + 1) * LANES]

    @pl.loop(0, win)
    def _(c):
        slopes = jnp.concatenate(
            [shifted[a, pl.ds(c, ROWS, stride=win), :] for a in range(padded // LANES)], 1).astype(jnp.bfloat16)
        for b in range(LANES // ROWS):
            moved = slopes[:, b * ROWS:b * ROWS + span]
            for a in range(span // LANES):
                at = pl.multiple_of(c * span + a * LANES + b * ROWS, ROWS)
                hankel[pl.ds(at, ROWS), :] = moved[:, a * LANES:(a + 1) * LANES]

    @pl.loop(1, chips)
    def _(step):
        from_chip(step).wait_recv()
        to_sibling(step).start()

    def widen(slot):
        rows = pl.ds(pl.multiple_of(slot * packed_rows, 8), packed_rows)
        for a in range(taps // LANES):
            wide[a, rows, :] = buf[slot, :, a * LANES:(a + 1) * LANES].astype(jnp.float32)

    @pl.loop(0, chips)
    def _(step):
        widen(near(step))

    @pl.loop(0, chips)
    def _(step):
        from_sibling(step).wait_recv()
        widen(near(step) + 1 - 2 * core)

    meta = wide[0, pl.ds(win, count, stride=packed_rows), :]
    lane = lax.broadcasted_iota(jnp.int32, (count, LANES), 1)
    offsets = jnp.sum(jnp.where(lane == win, meta, 0.0), 1, keepdims=True).astype(jnp.int32)

    def channel(c, total):
        low = wide[0, pl.ds(c, count, stride=packed_rows), :]
        high = wide[1, pl.ds(c, count, stride=packed_rows), :]
        move = jnp.sum(jnp.where(lane == c, meta, 0.0), 1, keepdims=True).astype(jnp.int32)
        move = jnp.broadcast_to(move, (count, LANES))
        part = move & (LANES - 1)
        index = (lane - part) & (LANES - 1)
        low = jnp.take_along_axis(low, index, 1)
        high = jnp.take_along_axis(high, index, 1)
        inside, late = lane >= part, move >= LANES
        own = jnp.broadcast_to(offsets, (count, LANES)) <= c
        first = jnp.where(inside, low, 0.0)
        second = jnp.where(inside, high, low)
        third = jnp.where(inside, 0.0, high)
        tiles = [jnp.where(late, 0.0, first), jnp.where(late, first, second),
                 jnp.where(late, second, third), jnp.where(late, third, 0.0)]
        here = jnp.concatenate([jnp.where(own, t, 0.0) for t in tiles], 1).astype(jnp.bfloat16)
        there = jnp.concatenate([jnp.where(own, 0.0, t) for t in tiles], 1).astype(jnp.bfloat16)
        both = jnp.concatenate([here, there], 0)
        block = hankel[pl.ds(pl.multiple_of(c * span, span), span), :]
        return total + jnp.dot(both, block, preferred_element_type=jnp.float32)

    total = lax.fori_loop(0, win, channel, jnp.zeros((2 * count, LANES), jnp.float32), unroll=2)

    r_out[...] = total[count:]
    send = pltpu.make_async_remote_copy(
        src_ref=r_out, dst_ref=r_in, send_sem=r_send, recv_sem=r_recv, device_id={"chan": before})
    send.start()

    @pl.loop(1, chips)
    def _(step):
        to_chip(step).wait_send()

    @pl.loop(0, chips)
    def _(step):
        to_sibling(step).wait_send()

    send.wait_recv()
    last = me == count - 1
    o_ref[0] = total[:count] + jnp.where(last, 0.0, r_in[...])
    send.wait_send()


def per_device(samples, templates, moveouts, offsets):
    win, slab = samples.shape
    taps = templates.shape[2]
    count = lax.axis_size("chan")
    lags = slab - taps - MOVE + 2
    chips = count // 2
    span = taps + MOVE
    padded = -(-(slab + 1) // LANES) * LANES
    packed_rows = win + ROWS
    vmem = pl.BlockSpec(memory_space=pltpu.VMEM)
    return pl.pallas_call(
        functools.partial(kernel, count),
        out_shape=jax.ShapeDtypeStruct((1, count, lags), jnp.float32),
        in_specs=[vmem, vmem, vmem, pl.BlockSpec(memory_space=pltpu.SMEM)],
        out_specs=vmem,
        scratch_shapes=[
            pltpu.VMEM((count, packed_rows, taps), jnp.bfloat16),
            pltpu.VMEM((padded // LANES, ROWS * win, LANES), jnp.float32),
            pltpu.VMEM((win * span, LANES), jnp.bfloat16),
            pltpu.VMEM((taps // LANES, count * packed_rows, LANES), jnp.float32),
            pltpu.VMEM((count, LANES), jnp.float32),
            pltpu.VMEM((count, LANES), jnp.float32),
            pltpu.SemaphoreType.DMA((chips,)),
            pltpu.SemaphoreType.DMA((chips,)),
            pltpu.SemaphoreType.DMA((chips,)),
            pltpu.SemaphoreType.DMA((chips,)),
            pltpu.SemaphoreType.DMA,
            pltpu.SemaphoreType.DMA,
        ],
        compiler_params=pltpu.CompilerParams(
            collective_id=0, has_side_effects=True, vmem_limit_bytes=48 * 2**20),
        cost_estimate=pl.CostEstimate(
            flops=4 * count * win * span * lags, bytes_accessed=4 * win * slab, transcendentals=0),
    )(samples, templates, moveouts, offsets)


def solution(mesh):
    in_specs = (P(("groups", "chan"), None), P("chan", None, None), P("chan", None), P("chan"))
    out_specs = P(("groups", "chan"), None, None)
    return jax.shard_map(
        per_device, mesh=mesh, in_specs=in_specs, out_specs=out_specs, check_vma=False
    )
```

time: 1780 us -> 32.9 us (0.02)
  matrix products: 1150 us -> 0 us
  local copies, waits for them, and re-layouts: 546 us -> 2.24 us
  blocking collectives: 48.9 us -> 0 us
  Pallas kernels: 0 us -> 29.7 us
  loops' own time: 27.6 us -> 0 us
    conv_general_dilated x16 -> x0, matrix products: 1150 us -> none  [correlate(): lax.conv_general_dilated(signal, kernel[None], (1,), 'VALID', dimension_n...]
    gather x16 -> x0, local copies, waits for them, and re-layouts: 384 us -> none  [shift_signal(): lax.dynamic_slice_in_dim(signal, amount, lag_count + tap_count - 1, 0)]
    dynamic_slice x80 -> x0, local copies, waits for them, and re-layouts: 158 us -> none  [the longest x32 146 us: single_template(): windows = lax.dynamic_slice_in_dim(blocks, offset, block_rows, 1)]
    all_gather x2 -> x0, blocking collectives: 42.1 us -> none  [the longest x1 24.7 us: per_device(): lax.all_gather(templates, 'chan', axis=0, tiled=True)]
    pallas_call x0 -> x1, Pallas kernels: none -> 29.7 us  [per_device(): pl.pallas_call(functools.partial(kernel, count), out_shape=jax.ShapeDtype...]
    another operation x1 -> x0, loops' own time: 27.6 us -> none  [per_device(): lax.map(single_template, (lax.all_gather(templates, 'chan', axis=0, tiled...]
  transfers between devices with their start and end apart: 1 -> 0, of which waited for: 1 -> 0; matrix products, arithmetic and copies ran while one was open for 0% -> 0% of each run, Pallas kernels for 0% -> 0%
where the time goes in v1:
time: 32.9 us; the launch traced here: 32.6 us
  Pallas kernels  29.7 us (90%)
  local copies, waits for them, and re-layouts  2.24 us (7%)
  between operations  0.69 us (2%)
    pallas_call x1, Pallas kernels, per_device(): pl.pallas_call(functools.partial(kernel, count), out_shape=jax.ShapeDtype...  29.7 us
    unnamed x7, local copies, waits for them, and re-layouts  2.24 us

profile of v1, /device:TPU:1, one launch (start us, length us, event | category | flops | bytes accessed | tf_op | source)
XLA Modules:
  0.0 32.6 jit_solution(1142936876990838458)
XLA Ops:
  0.0 0.0 copy-start.2
  0.7 0.0 copy-done.2
  0.7 0.0 copy-start
  0.7 0.9 %copy-done = bf16[64,638]{1,0:T(8,128)(2,1)S(1)} copy-done((bf16[64,638]{1,0:T(8,128)(2,1)S(1)}, bf16[64,638]{1,0:T(8,128)(2,1)}, u32[]{:S(2)}) %copy-start) | copy-done | bytes 81688
  1.6 0.0 copy-start.1
  1.6 0.8 %copy-done.1 = bf16[1,64,256]{2,1,0:T(8,128)(2,1)S(1)} copy-done((bf16[1,64,256]{2,1,0:T(8,128)(2,1)S(1)}, bf16[1,64,256]{2,1,0:T(8,128)(2,1)}, u32[]{:S(2)}) %copy-start.1) | copy-done | bytes 32792
  2.3 29.7 %shard_map.46 = f32[1,16,128]{2,1,0:T(8,128)S(1)} custom-call(bf16[64,638]{1,0:T(8,128)(2,1)S(1)} %copy-done, bf16[1,64,256]{2,1,0:T(8,128)(2,1)S(1)} %copy-done.1, s32[1,64]{1,0:T(1,128)S(1)} %copy-done.2, s32[1]{0:T(128)S(6)} %copy.6.off_ref), custom_call_target="tpu_custom_call" | custom-call | flops 268435456 | bytes 163328 | tf_op jit(solution)/shard_map/pallas_call | solution.py:181
  32.0 0.6 %copy.7 = f32[1,16,128]{2,1,0:T(8,128)} copy(f32[1,16,128]{2,1,0:T(8,128)S(1)} %shard_map.46) | data formatting | bytes 16384
Async XLA Ops:
  0.0 0.7 %copy-start.2 = (s32[1,64]{1,0:T(1,128)S(1)}, s32[1,64]{1,0:T(1,128)}, u32[]{:S(2)}) copy-start(s32[1,64]{1,0:T(1,128)} %m_ref.1) | copy-start | bytes 772
  0.7 0.9 %copy-start = (bf16[64,638]{1,0:T(8,128)(2,1)S(1)}, bf16[64,638]{1,0:T(8,128)(2,1)}, u32[]{:S(2)}) copy-start(bf16[64,638]{1,0:T(8,128)(2,1)} %x_ref.1) | copy-start | bytes 244996
  1.6 0.8 %copy-start.1 = (bf16[1,64,256]{2,1,0:T(8,128)(2,1)S(1)}, bf16[1,64,256]{2,1,0:T(8,128)(2,1)}, u32[]{:S(2)}) copy-start(bf16[1,64,256]{2,1,0:T(8,128)(2,1)} %h_ref.1) | copy-start | bytes 98308

commit v2 on v1

--- a/solution.py
+++ b/solution.py
@@ -92,7 +92,7 @@
         for a in range(padded // LANES):
             shifted[a, r * win:(r + 1) * win, :] = moved[:, a * LANES:(a + 1) * LANES]
 
-    @pl.loop(0, win)
+    @pl.loop(0, win, unroll=8)
     def _(c):
         slopes = jnp.concatenate(
             [shifted[a, pl.ds(c, ROWS, stride=win), :] for a in range(padded // LANES)], 1).astype(jnp.bfloat16)
@@ -147,7 +147,7 @@
         block = hankel[pl.ds(pl.multiple_of(c * span, span), span), :]
         return total + jnp.dot(both, block, preferred_element_type=jnp.float32)
 
-    total = lax.fori_loop(0, win, channel, jnp.zeros((2 * count, LANES), jnp.float32), unroll=2)
+    total = lax.fori_loop(0, win, channel, jnp.zeros((2 * count, LANES), jnp.float32), unroll=8)
 
     r_out[...] = total[count:]
     send = pltpu.make_async_remote_copy(

time: 32.9 us -> 23.2 us (0.71)
  Pallas kernels: 29.7 us -> 20 us
    pallas_call x1, Pallas kernels: 29.7 us -> 20 us  [per_device(): pl.pallas_call(functools.partial(kernel, count), out_shape=jax.ShapeDtype...]
where the time goes in v2:
time: 23.2 us; the launch traced here: 23 us
  Pallas kernels  20 us (86%)
  local copies, waits for them, and re-layouts  2.24 us (10%)
  between operations  0.69 us (3%)
    pallas_call x1, Pallas kernels, per_device(): pl.pallas_call(functools.partial(kernel, count), out_shape=jax.ShapeDtype...  20 us
    unnamed x7, local copies, waits for them, and re-layouts  2.24 us

profile of v2, /device:TPU:1, one launch (start us, length us, event | category | flops | bytes accessed | tf_op | source)
XLA Modules:
  0.0 23.0 jit_solution(11592018757596087258)
XLA Ops:
  0.0 0.0 copy-start.2
  0.7 0.0 copy-done.2
  0.7 0.0 copy-start
  0.7 0.9 %copy-done = bf16[64,638]{1,0:T(8,128)(2,1)S(1)} copy-done((bf16[64,638]{1,0:T(8,128)(2,1)S(1)}, bf16[64,638]{1,0:T(8,128)(2,1)}, u32[]{:S(2)}) %copy-start) | copy-done | bytes 81688
  1.6 0.0 copy-start.1
  1.6 0.8 %copy-done.1 = bf16[1,64,256]{2,1,0:T(8,128)(2,1)S(1)} copy-done((bf16[1,64,256]{2,1,0:T(8,128)(2,1)S(1)}, bf16[1,64,256]{2,1,0:T(8,128)(2,1)}, u32[]{:S(2)}) %copy-start.1) | copy-done | bytes 32792
  2.3 20.0 %shard_map.46 = f32[1,16,128]{2,1,0:T(8,128)S(1)} custom-call(bf16[64,638]{1,0:T(8,128)(2,1)S(1)} %copy-done, bf16[1,64,256]{2,1,0:T(8,128)(2,1)S(1)} %copy-done.1, s32[1,64]{1,0:T(1,128)S(1)} %copy-done.2, s32[1]{0:T(128)S(6)} %copy.6.off_ref), custom_call_target="tpu_custom_call" | custom-call | flops 268435456 | bytes 163328 | tf_op jit(solution)/shard_map/pallas_call | solution.py:181
  22.4 0.6 %copy.7 = f32[1,16,128]{2,1,0:T(8,128)} copy(f32[1,16,128]{2,1,0:T(8,128)S(1)} %shard_map.46) | data formatting | bytes 16384
Async XLA Ops:
  0.0 0.7 %copy-start.2 = (s32[1,64]{1,0:T(1,128)S(1)}, s32[1,64]{1,0:T(1,128)}, u32[]{:S(2)}) copy-start(s32[1,64]{1,0:T(1,128)} %m_ref.1) | copy-start | bytes 772
  0.7 0.9 %copy-start = (bf16[64,638]{1,0:T(8,128)(2,1)S(1)}, bf16[64,638]{1,0:T(8,128)(2,1)}, u32[]{:S(2)}) copy-start(bf16[64,638]{1,0:T(8,128)(2,1)} %x_ref.1) | copy-start | bytes 244996
  1.6 0.8 %copy-start.1 = (bf16[1,64,256]{2,1,0:T(8,128)(2,1)S(1)}, bf16[1,64,256]{2,1,0:T(8,128)(2,1)}, u32[]{:S(2)}) copy-start(bf16[1,64,256]{2,1,0:T(8,128)(2,1)} %h_ref.1) | copy-start | bytes 98308

commit v3 on v2

--- a/solution.py
+++ b/solution.py
@@ -92,7 +92,7 @@
         for a in range(padded // LANES):
             shifted[a, r * win:(r + 1) * win, :] = moved[:, a * LANES:(a + 1) * LANES]
 
-    @pl.loop(0, win, unroll=8)
+    @pl.loop(0, win, unroll=16)
     def _(c):
         slopes = jnp.concatenate(
             [shifted[a, pl.ds(c, ROWS, stride=win), :] for a in range(padded // LANES)], 1).astype(jnp.bfloat16)
@@ -147,7 +147,7 @@
         block = hankel[pl.ds(pl.multiple_of(c * span, span), span), :]
         return total + jnp.dot(both, block, preferred_element_type=jnp.float32)
 
-    total = lax.fori_loop(0, win, channel, jnp.zeros((2 * count, LANES), jnp.float32), unroll=8)
+    total = lax.fori_loop(0, win, channel, jnp.zeros((2 * count, LANES), jnp.float32), unroll=16)
 
     r_out[...] = total[count:]
     send = pltpu.make_async_remote_copy(

time: 23.2 us -> 22.6 us (0.974)
  Pallas kernels: 20 us -> 19.5 us
    pallas_call x1, Pallas kernels: 20 us -> 19.5 us  [per_device(): pl.pallas_call(functools.partial(kernel, count), out_shape=jax.ShapeDtype...]
where the time goes in v3:
time: 22.6 us; the launch traced here: 22.4 us
  Pallas kernels  19.5 us (86%)
  local copies, waits for them, and re-layouts  2.24 us (10%)
  between operations  0.69 us (3%)
    pallas_call x1, Pallas kernels, per_device(): pl.pallas_call(functools.partial(kernel, count), out_shape=jax.ShapeDtype...  19.5 us
    unnamed x7, local copies, waits for them, and re-layouts  2.24 us

profile of v3, /device:TPU:1, one launch (start us, length us, event | category | flops | bytes accessed | tf_op | source)
XLA Modules:
  0.0 22.4 jit_solution(16918823789530242987)
XLA Ops:
  0.0 0.0 copy-start.2
  0.7 0.0 copy-done.2
  0.7 0.0 copy-start
  0.7 0.9 %copy-done = bf16[64,638]{1,0:T(8,128)(2,1)S(1)} copy-done((bf16[64,638]{1,0:T(8,128)(2,1)S(1)}, bf16[64,638]{1,0:T(8,128)(2,1)}, u32[]{:S(2)}) %copy-start) | copy-done | bytes 81688
  1.6 0.0 copy-start.1
  1.6 0.8 %copy-done.1 = bf16[1,64,256]{2,1,0:T(8,128)(2,1)S(1)} copy-done((bf16[1,64,256]{2,1,0:T(8,128)(2,1)S(1)}, bf16[1,64,256]{2,1,0:T(8,128)(2,1)}, u32[]{:S(2)}) %copy-start.1) | copy-done | bytes 32792
  2.3 19.5 %shard_map.46 = f32[1,16,128]{2,1,0:T(8,128)S(1)} custom-call(bf16[64,638]{1,0:T(8,128)(2,1)S(1)} %copy-done, bf16[1,64,256]{2,1,0:T(8,128)(2,1)S(1)} %copy-done.1, s32[1,64]{1,0:T(1,128)S(1)} %copy-done.2, s32[1]{0:T(128)S(6)} %copy.6.off_ref), custom_call_target="tpu_custom_call" | custom-call | flops 268435456 | bytes 163328 | tf_op jit(solution)/shard_map/pallas_call | solution.py:181
  21.8 0.6 %copy.7 = f32[1,16,128]{2,1,0:T(8,128)} copy(f32[1,16,128]{2,1,0:T(8,128)S(1)} %shard_map.46) | data formatting | bytes 16384
Async XLA Ops:
  0.0 0.7 %copy-start.2 = (s32[1,64]{1,0:T(1,128)S(1)}, s32[1,64]{1,0:T(1,128)}, u32[]{:S(2)}) copy-start(s32[1,64]{1,0:T(1,128)} %m_ref.1) | copy-start | bytes 772
  0.7 0.9 %copy-start = (bf16[64,638]{1,0:T(8,128)(2,1)S(1)}, bf16[64,638]{1,0:T(8,128)(2,1)}, u32[]{:S(2)}) copy-start(bf16[64,638]{1,0:T(8,128)(2,1)} %x_ref.1) | copy-start | bytes 244996
  1.6 0.8 %copy-start.1 = (bf16[1,64,256]{2,1,0:T(8,128)(2,1)S(1)}, bf16[1,64,256]{2,1,0:T(8,128)(2,1)}, u32[]{:S(2)}) copy-start(bf16[1,64,256]{2,1,0:T(8,128)(2,1)} %h_ref.1) | copy-start | bytes 98308
